TPU v7x, 32 devices: a whole 2x2x4 slice. The times are simulated.
32 devices in a mesh: groups: 2 (over y), seq: 8 (over z, x), heads: 2 (over core).
Axes of the slice: x: 2, y: 2, z: 4, core: 2. Of those that a mesh axis runs over, the one named last changes fastest.
Arguments:
- queries: bfloat16 [4096, 2048], P(('groups', 'seq'), 'heads'), parts along dimension 0, may hold values from -180 to 180
- key_rows: bfloat16 [4096, 2048], P(('groups', 'seq'), 'heads'), parts along dimension 0, may hold values from -6 to 6
- value_rows: bfloat16 [4096, 2048], P(('groups', 'seq'), 'heads'), parts along dimension 0, may hold values from -19 to 19
- query_basis: bfloat16 [4096, 256], P(('groups', 'seq'), 'heads'), parts along dimension 0, may hold values from -6 to 6
- key_basis: bfloat16 [4096, 256], P(('groups', 'seq'), 'heads'), parts along dimension 0, may hold values from -6 to 6
- linear_gain: float32 [2048], P('heads'), may hold values from 0.25 to 1.75
Outputs:
- layer_output: bfloat16 [4096, 2048], P(('groups', 'seq'), 'heads'), parts along dimension 0
There are 2 independent parts, one for each index of `groups`. A program takes and returns all parts, laid end to end along the dimension named above; an argument that names none is the same for every part. Nothing has to cross between parts.
All inputs are finite; a program needn't handle non-finite values.
Results may differ from a plain program's by a relative error of at most 0.0075.
Values may be sent and summed in bfloat16 or wider, within the bound.
A program may use at most 320 MiB of HBM per device.

v0:
```python
import math

import jax
import jax.numpy as jnp
from jax import lax
from jax.sharding import PartitionSpec as P

DH = 128
FD = 16
WINDOW = 256


def passed_along(block, axis, distance):
    devices = range(lax.axis_size(axis))
    route = [(i - distance, i) for i in devices if i - distance in devices]
    return lax.ppermute(block, axis, route)


def carried_in(value, axis, join, neutral):
    place = lax.axis_index(axis)
    gathered = lax.all_gather(value.astype(jnp.bfloat16), axis)
    state = jnp.zeros_like(value) + jnp.asarray(neutral, value.dtype)

    def one(lap, state):
        return join(state, lax.dynamic_index_in_dim(gathered, lap, 0, False).astype(value.dtype))

    return lax.fori_loop(0, place, one, state)


def scaled_basis(basis):
    tokens = basis.shape[0]
    heads = basis.shape[1] // FD
    return basis.astype(jnp.float32).reshape(tokens, heads, FD).transpose(1, 2, 0) * FD ** (-0.25)


def full_features(basis):
    scaled = scaled_basis(basis)
    heads, width, tokens = scaled.shape
    second = (scaled[:, :, None, :] * scaled[:, None, :, :]).reshape(
        heads, width * width, tokens
    ) / math.sqrt(2.0)
    ones_row = jnp.ones((heads, 1, tokens), jnp.float32)
    return jnp.concatenate([ones_row, scaled, second], axis=1).astype(jnp.bfloat16)


def add_states(earlier, later):
    return earlier + later


def on_device(queries, key_rows, value_rows, query_basis, key_basis, linear_gain):
    tokens = queries.shape[0]
    heads = queries.shape[1] // DH
    blocks = tokens // WINDOW
    position = lax.axis_index("seq") * tokens
    tail = jnp.stack([key_rows, value_rows])
    before = passed_along(tail, "seq", 1)
    key_all = jnp.concatenate([before[0], key_rows], axis=0)
    value_all = jnp.concatenate([before[1], value_rows], axis=0)
    query_pos = jnp.arange(WINDOW, dtype=jnp.int32)[:, None]
    key_pos = jnp.arange(2 * WINDOW, dtype=jnp.int32)[None, :]
    inside = (key_pos >= query_pos) & (key_pos <= query_pos + WINDOW)

    def window_tile(tile_index):
        head_index = tile_index // blocks
        block_index = tile_index % blocks
        begin = block_index * WINDOW
        query_tile = lax.dynamic_slice(queries, (begin, head_index * DH), (WINDOW, DH))
        key_tile = lax.dynamic_slice(key_all, (begin, head_index * DH), (2 * WINDOW, DH))
        value_tile = lax.dynamic_slice(value_all, (begin, head_index * DH), (2 * WINDOW, DH))
        scores = lax.dot_general(
            query_tile, key_tile, (((1,), (1,)), ((), ())), preferred_element_type=jnp.float32
        ) / math.sqrt(DH)
        allowed = inside & (position + begin - WINDOW + key_pos >= 0)
        scores = jnp.where(allowed, scores, -1e30)
        row_top = jnp.max(scores, axis=-1, keepdims=True)
        expo = jnp.exp(scores - row_top)
        row_total = jnp.sum(expo, axis=-1, keepdims=True)
        return (
            jnp.dot(expo.astype(jnp.bfloat16), value_tile, preferred_element_type=jnp.float32)
            / row_total
        )

    tiles = lax.map(window_tile, jnp.arange(heads * blocks, dtype=jnp.int32))
    query_feats = full_features(query_basis)
    key_feats = full_features(key_basis)
    value_heads = value_rows.reshape(tokens, heads, DH)
    block_term = jnp.einsum(
        "hft,thd->hfd", key_feats, value_heads, preferred_element_type=jnp.float32
    )
    prior = carried_in(block_term, "seq", add_states, jnp.zeros_like(block_term))
    cross = jnp.einsum(
        "hft,hfd->htd", query_feats, prior.astype(jnp.bfloat16), preferred_element_type=jnp.float32
    )
    query_heads = query_basis.reshape(tokens, heads, FD)
    key_heads = key_basis.reshape(tokens, heads, FD)
    affinity = jnp.einsum(
        "thf,shf->hts", query_heads, key_heads, preferred_element_type=jnp.float32
    ) / math.sqrt(FD)
    causal = jnp.arange(tokens)[:, None] >= jnp.arange(tokens)[None, :]
    kernel = jnp.where(causal, 1.0 + affinity + affinity * affinity / 2.0, 0.0).astype(jnp.bfloat16)
    local_part = jnp.einsum("hts,shd->htd", kernel, value_heads, preferred_element_type=jnp.float32)
    linear_raw = cross + local_part
    scale_inv = lax.rsqrt(jnp.mean(linear_raw * linear_raw, axis=-1, keepdims=True) + 1e-05)
    linear_out = linear_raw * scale_inv * linear_gain.reshape(heads, 1, DH)
    combined = tiles + linear_out
    return combined.transpose(1, 0, 2).reshape(tokens, heads * DH).astype(jnp.bfloat16)


def solution(mesh):
    placed = (
        P(("groups", "seq"), "heads"),
        P(("groups", "seq"), "heads"),
        P(("groups", "seq"), "heads"),
        P(("groups", "seq"), "heads"),
        P(("groups", "seq"), "heads"),
        P("heads"),
    )
    return jax.shard_map(
        on_device,
        mesh=mesh,
        in_specs=placed,
        out_specs=P(("groups", "seq"), "heads"),
        check_vma=False,
    )
```

profile of v0, /device:TPU:26, one launch (start us, length us, event | category | flops | bytes accessed | tf_op | source)
XLA Modules:
  0.0 121.3 jit_solution(7813115168702155720)
XLA Ops:
  8.9 1.6 %convolution_convert_fusion = bf16[8,273,128]{2,1,0:T(8,128)(2,1)S(1)} fusion(bf16[256,8,128]{0,2,1:T(8,128)(2,1)} %bitcast.51, bf16[8,256,256]{2,1,0:T(8,128)(2,1)S(1)} %bitcast.50, bf16[8,16,256]{2,1,0:T(8,128)(2,1)S(1)} %convert.21, bf16[273]{0:T(512)(128)(2,1)S(1)} %pad.3.clone), kind=kOutput, calls=%fused_computation.30 | convolution fusion | flops 146764800 | bytes 2198050 | tf_op jit(solution)/shard_map/hft,thd->hfd/dot_general | solution.py:87
  12.6 1.3 %collective-permute-start = (bf16[2,256,1024]{2,1,0:T(8,128)(2,1)}, bf16[2,256,1024]{2,1,0:T(8,128)(2,1)}, u32[]{:S(2)}, u32[]{:S(2)}) collective-permute-start(bf16[2,256,1024]{2,1,0:T(8,128)(2,1)} %pad_maximum_fusion), channel_id=1, source_target_pairs={{0,2},{2,4},{4,6},{6,8},{8,10},{10,12},{12,14},{1,3},{3,5},{5,7},{... | collective-permute-start | bytes 3145736 | tf_op jit(solution)/shard_map/ppermute | solution.py:16
  14.6 1.9 %fusion.17 = f32[8,256,128]{1,2,0:T(8,128)S(1)} fusion(bf16[256,8,128]{0,2,1:T(8,128)(2,1)} %bitcast.52, bf16[256,8,16]{0,2,1:T(8,128)(2,1)S(1)} %bitcast.53, bf16[256,8,16]{0,2,1:T(8,128)(2,1)S(1)} %bitcast.54, pred[256,256]{1,0:T(8,128)(4,1)S(1)} %iota_compare_fusion.2), kind=kOutput, calls=%fused_computation.28 | convolution fusion | flops 154664960 | bytes 1769472 | tf_op jit(solution)/shard_map/hts,shd->htd/dot_general | solution.py:101
  16.6 29.1 %collective-permute-done = bf16[2,256,1024]{2,1,0:T(8,128)(2,1)} collective-permute-done((bf16[2,256,1024]{2,1,0:T(8,128)(2,1)}, bf16[2,256,1024]{2,1,0:T(8,128)(2,1)}, u32[]{:S(2)}, u32[]{:S(2)}) %collective-permute-start) | collective-permute-done | bytes 1048608 | tf_op jit(solution)/shard_map/ppermute | solution.py:16
  45.7 1.3 %slice_bitcast_fusion = (bf16[256,1024]{1,0:T(8,128)(2,1)S(1)}, bf16[256,1024]{1,0:T(8,128)(2,1)S(1)}) fusion(bf16[2,256,1024]{2,1,0:T(8,128)(2,1)} %collective-permute-done), kind=kLoop, calls=%fused_computation.52 | loop fusion | bytes 2097152 | tf_op jit(solution)/shard_map/squeeze | solution.py:58
  46.9 1.5 %pad_maximum_fusion.1 = (bf16[512,1024]{1,0:T(8,128)(2,1)}, bf16[512,1024]{1,0:T(8,128)(2,1)}) fusion(bf16[256,1024]{1,0:T(8,128)(2,1)S(1)} %copy-done.1, bf16[256,1024]{1,0:T(8,128)(2,1)S(1)} %get-tuple-element.285, bf16[256,1024]{1,0:T(8,128)(2,1)S(1)} %copy-done, bf16[256,1024]{1,0:T(8,128)(2,1)S(1)} %get-tuple-element.284), kind=kLoop, calls=%fused_computation.40 | loop fusion | flops 4194304 | bytes 4194304 | tf_op jit(solution)/shard_map/concatenate | solution.py:57
  48.5 38.0 %while.27 = (s32[]{:T(128)}, f32[8,256,128]{1,2,0:T(8,128)}, s32[]{:T(128)}, s32[8]{0:T(128)S(1)}, bf16[256,1024]{1,0:T(8,128)(2,1)}, /*index=5*/bf16[512,1024]{...) while((s32[]{:T(128)}, f32[8,256,128]{1,2,0:T(8,128)}, ...), condition=%wide.region_3.4_spmd.clone, body=%wide.region_0.3_spmd.clone.sunk | while | flops 68583936 | bytes 2564791 | solution.py:83
  49.7 1.3 %fusion.52 = (f32[256]{0:T(256)S(1)}, f32[256,512]{1,0:T(8,128)S(1)}) fusion(bf16[512,1024]{1,0:T(8,128)(2,1)} %get-tuple-element.398, s32[]{:T(128)S(6)} %select_n.55, bf16[256,1024]{1,0:T(8,128)(2,1)} %get-tuple-element.397, pred[512]{0:T(512)(128)(4,1)S(1)} %compare_reduce_fusion.2, s32[256]{0:T(256)S(1)} %get-tuple-element.400), kind=kOutput, calls=%fused_computation.65.clone.1 | convolution fusion | flops 34471680 | bytes 724480 | tf_op jit(solution)/shard_map/while/body/eval_jaxpr/dot_general | solution.py:70
  51.2 1.2 fusion.54
  54.5 1.3 %fusion.52 = (f32[256]{0:T(256)S(1)}, f32[256,512]{1,0:T(8,128)S(1)}) fusion(bf16[512,1024]{1,0:T(8,128)(2,1)} %get-tuple-element.398, s32[]{:T(128)S(6)} %select_n.55, bf16[256,1024]{1,0:T(8,128)(2,1)} %get-tuple-element.397, pred[512]{0:T(512)(128)(4,1)S(1)} %compare_reduce_fusion.2, s32[256]{0:T(256)S(1)} %get-tuple-element.400), kind=kOutput, calls=%fused_computation.65.clone.1 | convolution fusion | flops 34471680 | bytes 724480 | tf_op jit(solution)/shard_map/while/body/eval_jaxpr/dot_general | solution.py:70
  56.0 1.2 fusion.54
  59.2 1.3 %fusion.52 = (f32[256]{0:T(256)S(1)}, f32[256,512]{1,0:T(8,128)S(1)}) fusion(bf16[512,1024]{1,0:T(8,128)(2,1)} %get-tuple-element.398, s32[]{:T(128)S(6)} %select_n.55, bf16[256,1024]{1,0:T(8,128)(2,1)} %get-tuple-element.397, pred[512]{0:T(512)(128)(4,1)S(1)} %compare_reduce_fusion.2, s32[256]{0:T(256)S(1)} %get-tuple-element.400), kind=kOutput, calls=%fused_computation.65.clone.1 | convolution fusion | flops 34471680 | bytes 724480 | tf_op jit(solution)/shard_map/while/body/eval_jaxpr/dot_general | solution.py:70
  60.7 1.2 fusion.54
  64.0 1.3 %fusion.52 = (f32[256]{0:T(256)S(1)}, f32[256,512]{1,0:T(8,128)S(1)}) fusion(bf16[512,1024]{1,0:T(8,128)(2,1)} %get-tuple-element.398, s32[]{:T(128)S(6)} %select_n.55, bf16[256,1024]{1,0:T(8,128)(2,1)} %get-tuple-element.397, pred[512]{0:T(512)(128)(4,1)S(1)} %compare_reduce_fusion.2, s32[256]{0:T(256)S(1)} %get-tuple-element.400), kind=kOutput, calls=%fused_computation.65.clone.1 | convolution fusion | flops 34471680 | bytes 724480 | tf_op jit(solution)/shard_map/while/body/eval_jaxpr/dot_general | solution.py:70
  65.5 1.2 fusion.54
  68.7 1.3 %fusion.52 = (f32[256]{0:T(256)S(1)}, f32[256,512]{1,0:T(8,128)S(1)}) fusion(bf16[512,1024]{1,0:T(8,128)(2,1)} %get-tuple-element.398, s32[]{:T(128)S(6)} %select_n.55, bf16[256,1024]{1,0:T(8,128)(2,1)} %get-tuple-element.397, pred[512]{0:T(512)(128)(4,1)S(1)} %compare_reduce_fusion.2, s32[256]{0:T(256)S(1)} %get-tuple-element.400), kind=kOutput, calls=%fused_computation.65.clone.1 | convolution fusion | flops 34471680 | bytes 724480 | tf_op jit(solution)/shard_map/while/body/eval_jaxpr/dot_general | solution.py:70
  70.2 1.2 fusion.54
  73.5 1.3 %fusion.52 = (f32[256]{0:T(256)S(1)}, f32[256,512]{1,0:T(8,128)S(1)}) fusion(bf16[512,1024]{1,0:T(8,128)(2,1)} %get-tuple-element.398, s32[]{:T(128)S(6)} %select_n.55, bf16[256,1024]{1,0:T(8,128)(2,1)} %get-tuple-element.397, pred[512]{0:T(512)(128)(4,1)S(1)} %compare_reduce_fusion.2, s32[256]{0:T(256)S(1)} %get-tuple-element.400), kind=kOutput, calls=%fused_computation.65.clone.1 | convolution fusion | flops 34471680 | bytes 724480 | tf_op jit(solution)/shard_map/while/body/eval_jaxpr/dot_general | solution.py:70
  75.0 1.2 fusion.54
  78.2 1.3 %fusion.52 = (f32[256]{0:T(256)S(1)}, f32[256,512]{1,0:T(8,128)S(1)}) fusion(bf16[512,1024]{1,0:T(8,128)(2,1)} %get-tuple-element.398, s32[]{:T(128)S(6)} %select_n.55, bf16[256,1024]{1,0:T(8,128)(2,1)} %get-tuple-element.397, pred[512]{0:T(512)(128)(4,1)S(1)} %compare_reduce_fusion.2, s32[256]{0:T(256)S(1)} %get-tuple-element.400), kind=kOutput, calls=%fused_computation.65.clone.1 | convolution fusion | flops 34471680 | bytes 724480 | tf_op jit(solution)/shard_map/while/body/eval_jaxpr/dot_general | solution.py:70
  79.7 1.2 fusion.54
  82.9 1.3 %fusion.52 = (f32[256]{0:T(256)S(1)}, f32[256,512]{1,0:T(8,128)S(1)}) fusion(bf16[512,1024]{1,0:T(8,128)(2,1)} %get-tuple-element.398, s32[]{:T(128)S(6)} %select_n.55, bf16[256,1024]{1,0:T(8,128)(2,1)} %get-tuple-element.397, pred[512]{0:T(512)(128)(4,1)S(1)} %compare_reduce_fusion.2, s32[256]{0:T(256)S(1)} %get-tuple-element.400), kind=kOutput, calls=%fused_computation.65.clone.1 | convolution fusion | flops 34471680 | bytes 724480 | tf_op jit(solution)/shard_map/while/body/eval_jaxpr/dot_general | solution.py:70
  86.4 16.6 %all-gather.3.cloned.1.call-done = bf16[64,273,128]{2,0,1:T(8,128)(2,1)} async-done(((bf16[8,273,128]{2,0,1:T(8,128)(2,1)}), bf16[64,273,128]{2,0,1:T(8,128)(2,1)}) %all-gather.3.cloned.1.call-update) | async-done | bytes 4472848 | tf_op jit(solution)/shard_map/all_gather | solution.py:21
  103.1 9.0 %while.26 = (s32[]{:T(128)}, f32[8,273,128]{2,1,0:T(8,128)S(1)}, s32[]{:T(128)}, bf16[8,8,273,128]{3,1,0,2:T(8,128)(2,1)}, s32[]{:T(128)}, /*index=5*/s32[]{:T(128)}, s32[]{:T(128)}) while((s32[]{:T(128)}, f32[8,273,128]{2,1,0:T(8,128)S(1)}, s32[]{:T(128)}, bf16[8,8,273,128]{3,1,0,2:T(8,128)(2,1)}, s32[]{:T(128)}, /*index=5*/s32[]{:T(128)}, ...), condition=%wide.region_5.6_spmd, body=%wide.region_4.5_spmd.sunk | while | flops 559109 | bytes 3913843 | solution.py:27
  (92 shorter events, 30.2 us)
Async XLA Ops:
  6.5 1.4 %copy-start = (bf16[256,1024]{1,0:T(8,128)(2,1)S(1)}, bf16[256,1024]{1,0:T(8,128)(2,1)}, u32[]{:S(2)}) copy-start(bf16[256,1024]{1,0:T(8,128)(2,1)} %param.12) | copy-start | bytes 1572868
  6.5 96.4 %all-gather.3.cloned.1.call-start = ((), (), s32[]{:S(2)}) async-start(), calls=%async_computation | async-start | bytes 5031936 | tf_op jit(solution)/shard_map/all_gather | solution.py:21
  8.9 2.6 %copy-start.1 = (bf16[256,1024]{1,0:T(8,128)(2,1)S(1)}, bf16[256,1024]{1,0:T(8,128)(2,1)}, u32[]{:S(2)}) copy-start(bf16[256,1024]{1,0:T(8,128)(2,1)} %param.11) | copy-start | bytes 1572868
  10.6 3.3 %copy-start.3 = (bf16[256,128]{1,0:T(8,128)(2,1)S(1)}, bf16[256,128]{1,0:T(8,128)(2,1)}, u32[]{:S(2)}) copy-start(bf16[256,128]{1,0:T(8,128)(2,1)} %param.13) | copy-start | bytes 196612
  10.6 3.4 %copy-start.4 = (bf16[256,128]{1,0:T(8,128)(2,1)S(1)}, bf16[256,128]{1,0:T(8,128)(2,1)}, u32[]{:S(2)}) copy-start(bf16[256,128]{1,0:T(8,128)(2,1)} %param.14) | copy-start | bytes 196612
  12.6 33.1 %collective-permute-start = (bf16[2,256,1024]{2,1,0:T(8,128)(2,1)}, bf16[2,256,1024]{2,1,0:T(8,128)(2,1)}, u32[]{:S(2)}, u32[]{:S(2)}) collective-permute-start(bf16[2,256,1024]{2,1,0:T(8,128)(2,1)} %pad_maximum_fusion), channel_id=1, source_target_pairs={{0,2},{2,4},{4,6},{6,8},{8,10},{10,12},{12,14},{1,3},{3,5},{5,7},{... | collective-permute-start | bytes 3145736 | tf_op jit(solution)/shard_map/ppermute | solution.py:16
  112.0 1.2 %copy-start.2 = (f32[8,256,128]{1,2,0:T(8,128)S(1)}, f32[8,256,128]{1,2,0:T(8,128)}, u32[]{:S(2)}) copy-start(f32[8,256,128]{1,2,0:T(8,128)} %get-tuple-element.232) | copy-start | bytes 3145732
  112.1 1.2 %copy-start.5 = (f32[1024]{0:T(1024)S(1)}, f32[1024]{0:T(1024)}, u32[]{:S(2)}) copy-start(f32[1024]{0:T(1024)} %param.15) | copy-start | bytes 12292
Sparse Core Ops, SparseCore 0:
  11.6 91.3 all-gather.2
where the time goes:
time: 122 us; the launch traced here: 121 us
  waiting for transfers between devices  45.6 us (37%)
  matrix products  24.1 us (20%)
  local copies, waits for them, and re-layouts  23.5 us (19%)
  between operations  13.6 us (11%)
  other arithmetic  7.5 us (6%)
  loops' own time  5.63 us (5%)
  starting transfers between devices  1.28 us (1%)
    ppermute x1, waiting for transfers between devices, passed_along(): return lax.ppermute(block, axis, route)  29.1 us
    all_gather x1, waiting for transfers between devices, carried_in(): gathered = lax.all_gather(value.astype(jnp.bfloat16), axis)  16.6 us
    dot_general x8, matrix products, window_tile(): lax.dot_general(query_tile, key_tile, (((1,), (1,)), ((), ())), preferred...  10.2 us
    dot_general x8, matrix products, window_tile(): jnp.dot(expo.astype(jnp.bfloat16), value_tile, preferred_element_type=jnp...  9.57 us
    dynamic_slice x7, local copies, waits for them, and re-layouts, one(): lax.dynamic_index_in_dim(gathered, lap, 0, False).astype(value.dtype)  7.67 us
    dynamic_update_slice x16, local copies, waits for them, and re-layouts, on_device(): tiles = lax.map(window_tile, jnp.arange(heads * blocks, dtype=jnp.int32))  6.07 us
    another operation x1, loops' own time, on_device(): tiles = lax.map(window_tile, jnp.arange(heads * blocks, dtype=jnp.int32))  5.38 us
    dynamic_slice x8, local copies, waits for them, and re-layouts, on_device(): tiles = lax.map(window_tile, jnp.arange(heads * blocks, dtype=jnp.int32))  4.66 us
  transfers between devices with their start and end apart: 2, of which 2 were waited for; matrix products, arithmetic and copies ran while one was open for 32% of the time, Pallas kernels for 0%

commit v1 on v0

v1 whole, which is shorter than its diff:
```python
import functools
import math

import jax
import jax.numpy as jnp
from jax import lax
from jax.experimental import pallas as pl
from jax.experimental.pallas import tpu as pltpu
from jax.sharding import PartitionSpec as P

DH = 128
FD = 16
ROWS = 160
ONE = 136
LIN = 144
NEG = -1e30
F32 = jnp.float32
BF16 = jnp.bfloat16


def dot_nn(a, b):
    return lax.dot_general(a, b, (((1,), (0,)), ((), ())), preferred_element_type=F32)


def dot_nt(a, b):
    return lax.dot_general(a, b, (((1,), (1,)), ((), ())), preferred_element_type=F32)


def pair_places(c):
    i = c % FD
    j = (i + c // FD) % FD
    return i, j


def entry_scale(c, doubled):
    pair = 0.25 / math.sqrt(2.0)
    off = 2.0 * pair if doubled else pair
    scale = jnp.where(c < FD, pair, off)
    scale = jnp.where(c >= ONE, 0.0, scale)
    scale = jnp.where(c == ONE, 1.0, scale)
    return jnp.where(c >= LIN, 0.5, scale).astype(F32)


def kernel(n, heads, q_ref, k_ref, v_ref, qb_ref, kb_ref, gain_ref, out_ref,
           khalo, vhalo, prior, onward, state, qfeat, top, total, owin, lin,
           ksend, vsend, psend, krecv, vrecv, precv):
    me = lax.axis_index("seq")
    tokens = q_ref.shape[0]
    has_next = me < n - 1
    has_prev = me > 0
    nxt = {"seq": jnp.minimum(me + 1, n - 1)}
    prv = {"seq": jnp.maximum(me - 1, 0)}

    barrier = pltpu.get_barrier_semaphore()

    @pl.when(has_prev)
    def _():
        pl.semaphore_signal(barrier, inc=1, device_id=prv, device_id_type=pl.DeviceIdType.MESH)

    @pl.when(me == 0)
    def _():
        khalo[...] = jnp.zeros_like(khalo)
        vhalo[...] = jnp.zeros_like(vhalo)
        prior[...] = jnp.zeros_like(prior)

    @pl.when(has_next)
    def _():
        pl.semaphore_wait(barrier, 1)

    def cols(h):
        return pl.ds(pl.multiple_of(h * DH, DH), DH)

    def kcopy(h):
        return pltpu.make_async_remote_copy(
            src_ref=k_ref.at[:, cols(h)], dst_ref=khalo.at[h], send_sem=ksend.at[h],
            recv_sem=krecv.at[h], device_id=nxt, device_id_type=pl.DeviceIdType.MESH)

    def vcopy(h):
        return pltpu.make_async_remote_copy(
            src_ref=v_ref.at[:, cols(h)], dst_ref=vhalo.at[h], send_sem=vsend.at[h],
            recv_sem=vrecv.at[h], device_id=nxt, device_id_type=pl.DeviceIdType.MESH)

    def pcopy(h):
        return pltpu.make_async_remote_copy(
            src_ref=onward.at[h], dst_ref=prior.at[h], send_sem=psend.at[h],
            recv_sem=precv.at[h], device_id=nxt, device_id_type=pl.DeviceIdType.MESH)

    def each_head(body):
        def step(h, carry):
            body(h)
            return carry
        lax.fori_loop(0, heads, step, 0)

    crow = lax.broadcasted_iota(jnp.int32, (ROWS, heads * FD), 0)
    lane = lax.broadcasted_iota(jnp.int32, (ROWS, heads * FD), 1)
    i, j = pair_places(crow)
    first = jnp.where(crow == ONE, -1, lane - i)
    second = jnp.where(crow >= ONE, -1, lane - j)
    ccol = lax.broadcasted_iota(jnp.int32, (ROWS, 1), 0)
    kscale = entry_scale(ccol, False)
    kone_a = jnp.where(ccol == ONE, 1.0, 0.0).astype(F32)
    kone_b = jnp.where(ccol >= ONE, 1.0, 0.0).astype(F32)

    def own_state(h):
        pick_a = jnp.where(first == h * FD, 1.0, 0.0).astype(BF16)
        pick_b = jnp.where(second == h * FD, 1.0, 0.0).astype(BF16)
        a = dot_nt(pick_a, kb_ref[...]) + kone_a
        b = dot_nt(pick_b, kb_ref[...]) + kone_b
        feats = (a * b * kscale).astype(BF16)
        got = dot_nn(feats, v_ref[:, cols(h)])
        state[h] = got

        @pl.when(me == 0)
        def _():
            onward[h] = got.astype(onward.dtype)
            pcopy(h).start()

    each_head(own_state)

    @pl.when(has_next)
    def _():
        def send(h):
            kcopy(h).start()
            vcopy(h).start()
        each_head(send)

    def chain(h):
        pcopy(h).wait_recv()

        @pl.when(has_next)
        def _():
            onward[h] = (prior[h].astype(F32) + state[h]).astype(onward.dtype)
            pcopy(h).start()

    early = n // 2 - 1

    @pl.when(has_prev & (me <= early))
    def _():
        each_head(chain)

    row = lax.broadcasted_iota(jnp.int32, (tokens, tokens), 0)
    col = lax.broadcasted_iota(jnp.int32, (tokens, tokens), 1)
    qrow = lax.broadcasted_iota(jnp.int32, (heads * FD, ROWS), 1)
    qlane = lax.broadcasted_iota(jnp.int32, (heads * FD, ROWS), 0)
    qi, qj = pair_places(qrow)
    qfirst = jnp.where(qrow == ONE, -1, qlane - qi)
    qsecond = jnp.where(qrow >= ONE, -1, qlane - qj)
    clane = lax.broadcasted_iota(jnp.int32, (1, ROWS), 1)
    qscale = entry_scale(clane, True)
    qone_a = jnp.where(clane == ONE, 1.0, 0.0).astype(F32)
    qone_b = jnp.where(clane >= ONE, 1.0, 0.0).astype(F32)
    blane = lax.broadcasted_iota(jnp.int32, (1, heads * FD), 1) // FD
    root = 1.0 / math.sqrt(DH)

    def local(h):
        v = v_ref[:, cols(h)]
        scores = dot_nt(q_ref[:, cols(h)], k_ref[:, cols(h)]) * root
        scores = jnp.where(col <= row, scores, NEG)
        peak = jnp.max(scores, axis=-1, keepdims=True)
        expo = jnp.exp(scores - peak)
        top[h] = peak
        total[h] = jnp.sum(expo, axis=-1, keepdims=True)
        owin[h] = dot_nn(expo.astype(BF16), v)
        qb = qb_ref[...]
        mine = jnp.where(blane == h, 1.0, 0.0).astype(BF16)
        w = dot_nt(qb * mine, kb_ref[...]) * (1.0 / math.sqrt(FD))
        kern = jnp.where(col <= row, 1.0 + w + w * w * 0.5, 0.0).astype(BF16)
        lin[h] = dot_nn(kern, v)
        pick_a = jnp.where(qfirst == h * FD, 1.0, 0.0).astype(BF16)
        pick_b = jnp.where(qsecond == h * FD, 1.0, 0.0).astype(BF16)
        a = dot_nn(qb, pick_a) + qone_a
        b = dot_nn(qb, pick_b) + qone_b
        qfeat[h] = (a * b * qscale).astype(BF16)

    each_head(local)

    @pl.when(me > early)
    def _():
        each_head(chain)

    reach = jnp.where(has_prev, 0, tokens)

    def finish(h):
        @pl.when(has_prev)
        def _():
            kcopy(h).wait_recv()
            vcopy(h).wait_recv()

        scores = dot_nt(q_ref[:, cols(h)], khalo[h]) * root
        scores = jnp.where(col >= row + reach, scores, NEG)
        before = top[h]
        peak = jnp.maximum(before, jnp.max(scores, axis=-1, keepdims=True))
        expo = jnp.exp(scores - peak)
        shrink = jnp.exp(before - peak)
        full = total[h] * shrink + jnp.sum(expo, axis=-1, keepdims=True)
        window = (owin[h] * shrink + dot_nn(expo.astype(BF16), vhalo[h])) / full
        raw = lin[h] + dot_nn(qfeat[h], prior[h].astype(BF16))
        inv = lax.rsqrt(jnp.mean(raw * raw, axis=-1, keepdims=True) + 1e-05)
        out_ref[:, cols(h)] = (window + raw * inv * gain_ref[:, cols(h)]).astype(BF16)

    each_head(finish)

    @pl.when(has_next)
    def _():
        def sent(h):
            kcopy(h).wait_send()
            vcopy(h).wait_send()
            pcopy(h).wait_send()
        each_head(sent)


def solution(mesh):
    n = mesh.shape["seq"]
    carried = BF16 if n <= 16 else F32

    def on_device(queries, key_rows, value_rows, query_basis, key_basis, linear_gain):
        tokens, width = queries.shape
        heads = width // DH
        vmem = pl.BlockSpec(memory_space=pltpu.VMEM)
        dma = pltpu.SemaphoreType.DMA((heads,))
        flops = 2 * tokens * heads * DH * (4 * tokens + tokens + 2 * ROWS + 4 * ROWS)
        return pl.pallas_call(
            functools.partial(kernel, n, heads),
            out_shape=jax.ShapeDtypeStruct((tokens, width), BF16),
            in_specs=[vmem] * 6,
            out_specs=vmem,
            scratch_shapes=[
                pltpu.VMEM((heads, tokens, DH), BF16),
                pltpu.VMEM((heads, tokens, DH), BF16),
                pltpu.VMEM((heads, ROWS, DH), carried),
                pltpu.VMEM((heads, ROWS, DH), carried),
                pltpu.VMEM((heads, ROWS, DH), F32),
                pltpu.VMEM((heads, tokens, ROWS), BF16),
                pltpu.VMEM((heads, tokens, 1), F32),
                pltpu.VMEM((heads, tokens, 1), F32),
                pltpu.VMEM((heads, tokens, DH), F32),
                pltpu.VMEM((heads, tokens, DH), F32),
                dma, dma, dma, dma, dma, dma,
            ],
            compiler_params=pltpu.CompilerParams(
                collective_id=0, has_side_effects=True, vmem_limit_bytes=40 * 2**20),
            cost_estimate=pl.CostEstimate(
                flops=flops, bytes_accessed=8 * tokens * width, transcendentals=2 * tokens * tokens * heads),
        )(queries, key_rows, value_rows, query_basis, key_basis, linear_gain.reshape(1, width))

    rows = P(("groups", "seq"), "heads")
    return jax.shard_map(
        on_device,
        mesh=mesh,
        in_specs=(rows, rows, rows, rows, rows, P("heads")),
        out_specs=rows,
        check_vma=False,
    )
```

time: 122 us -> 62.7 us (0.51)
  Pallas kernels: 0 us -> 56 us
  waiting for transfers between devices: 45.6 us -> 0 us
  matrix products: 24.1 us -> 0 us
  local copies, waits for them, and re-layouts: 23.5 us -> 6.28 us
  between operations: 13.6 us -> 0.02 us
  other arithmetic: 7.5 us -> 0 us
  loops' own time: 5.63 us -> 0 us
  starting transfers between devices: 1.28 us -> 0 us
    pallas_call x0 -> x1, Pallas kernels: none -> 56 us  [on_device(): pl.pallas_call(functools.partial(kernel, n, heads), out_shape=jax.ShapeDt...]
    ppermute x1 -> x0, waiting for transfers between devices: 29.1 us -> none  [passed_along(): return lax.ppermute(block, axis, route)]
    dot_general x19 -> x0, matrix products: 24.1 us -> none  [the longest x8 10.2 us: window_tile(): lax.dot_general(query_tile, key_tile, (((1,), (1,)), ((), ())), preferred...]
    all_gather x1 -> x0, waiting for transfers between devices: 16.6 us -> none  [carried_in(): gathered = lax.all_gather(value.astype(jnp.bfloat16), axis)]
    dynamic_slice x15 -> x0, local copies, waits for them, and re-layouts: 12.3 us -> none  [the longest x7 7.67 us: one(): lax.dynamic_index_in_dim(gathered, lap, 0, False).astype(value.dtype)]
    dynamic_update_slice x16 -> x0, local copies, waits for them, and re-layouts: 6.07 us -> none  [on_device(): tiles = lax.map(window_tile, jnp.arange(heads * blocks, dtype=jnp.int32))]
    another operation x2 -> x0, loops' own time: 5.63 us -> none  [the longest x1 5.38 us: on_device(): tiles = lax.map(window_tile, jnp.arange(heads * blocks, dtype=jnp.int32))]
    unnamed x14 -> x13, local copies, waits for them, and re-layouts: 0.71 us -> 6.28 us
  transfers between devices with their start and end apart: 2 -> 0, of which waited for: 2 -> 0; matrix products, arithmetic and copies ran while one was open for 32% -> 0% of each run, Pallas kernels for 0% -> 0%
where the time goes in v1:
time: 62.7 us; the launch traced here: 62.3 us
  Pallas kernels  56 us (89%)
  local copies, waits for them, and re-layouts  6.28 us (10%)
    pallas_call x1, Pallas kernels, on_device(): pl.pallas_call(functools.partial(kernel, n, heads), out_shape=jax.ShapeDt...  56 us
    unnamed x13, local copies, waits for them, and re-layouts  6.28 us

profile of v1, /device:TPU:26, one launch (start us, length us, event | category | flops | bytes accessed | tf_op | source)
XLA Modules:
  0.0 62.3 jit_solution(14337714296880151351)
XLA Ops:
  0.0 0.0 copy-start
  0.0 1.0 %copy-done = bf16[256,1024]{1,0:T(8,128)(2,1)S(1)} copy-done((bf16[256,1024]{1,0:T(8,128)(2,1)S(1)}, bf16[256,1024]{1,0:T(8,128)(2,1)}, u32[]{:S(2)}) %copy-start) | copy-done | bytes 524312
  1.0 0.0 copy-start.1
  1.0 1.0 %copy-done.1 = bf16[256,1024]{1,0:T(8,128)(2,1)S(1)} copy-done((bf16[256,1024]{1,0:T(8,128)(2,1)S(1)}, bf16[256,1024]{1,0:T(8,128)(2,1)}, u32[]{:S(2)}) %copy-start.1) | copy-done | bytes 524312
  2.1 0.0 copy-start.2
  2.1 1.0 %copy-done.2 = bf16[256,1024]{1,0:T(8,128)(2,1)S(1)} copy-done((bf16[256,1024]{1,0:T(8,128)(2,1)S(1)}, bf16[256,1024]{1,0:T(8,128)(2,1)}, u32[]{:S(2)}) %copy-start.2) | copy-done | bytes 524312
  3.1 0.0 copy-start.3
  3.1 0.8 %copy-done.3 = bf16[256,128]{1,0:T(8,128)(2,1)S(1)} copy-done((bf16[256,128]{1,0:T(8,128)(2,1)S(1)}, bf16[256,128]{1,0:T(8,128)(2,1)}, u32[]{:S(2)}) %copy-start.3) | copy-done | bytes 65560
  4.0 0.0 copy-start.4
  4.0 0.8 %copy-done.4 = bf16[256,128]{1,0:T(8,128)(2,1)S(1)} copy-done((bf16[256,128]{1,0:T(8,128)(2,1)S(1)}, bf16[256,128]{1,0:T(8,128)(2,1)}, u32[]{:S(2)}) %copy-start.4) | copy-done | bytes 65560
  4.8 0.0 copy-start.5
  4.8 0.7 %copy-done.5 = f32[1024]{0:T(1024)S(1)} copy-done((f32[1024]{0:T(1024)S(1)}, f32[1024]{0:T(1024)}, u32[]{:S(2)}) %copy-start.5) | copy-done | bytes 4120
  5.5 56.0 %shard_map.64 = bf16[256,1024]{1,0:T(8,128)(2,1)S(1)} custom-call(bf16[256,1024]{1,0:T(8,128)(2,1)S(1)} %copy-done, bf16[256,1024]{1,0:T(8,128)(2,1)S(1)} %copy-done.1, bf16[256,1024]{1,0:T(8,128)(2,1)S(1)} %copy-done.2, bf16[256,128]{1,0:T(8,128)(2,1)S(1)} %copy-done.3, bf16[256,128]{1,0:T(8,128)(2,1)S(1)} %copy-done.4, f32[1,1024]{1,0:T(1,128)S(1)} %bitcast.1), custom_call_target="tpu_custom_call" | custom-call | flops 1174405120 | bytes 2097152 | tf_op jit(solution)/shard_map/pallas_call | solution.py:222
  61.5 0.8 %copy.8 = bf16[256,1024]{1,0:T(8,128)(2,1)} copy(bf16[256,1024]{1,0:T(8,128)(2,1)S(1)} %shard_map.64) | data formatting | bytes 1048576
Async XLA Ops:
  0.0 1.0 %copy-start = (bf16[256,1024]{1,0:T(8,128)(2,1)S(1)}, bf16[256,1024]{1,0:T(8,128)(2,1)}, u32[]{:S(2)}) copy-start(bf16[256,1024]{1,0:T(8,128)(2,1)} %q_ref.1) | copy-start | bytes 1572868
  1.0 1.0 %copy-start.1 = (bf16[256,1024]{1,0:T(8,128)(2,1)S(1)}, bf16[256,1024]{1,0:T(8,128)(2,1)}, u32[]{:S(2)}) copy-start(bf16[256,1024]{1,0:T(8,128)(2,1)} %k_ref.1) | copy-start | bytes 1572868
  2.1 1.0 %copy-start.2 = (bf16[256,1024]{1,0:T(8,128)(2,1)S(1)}, bf16[256,1024]{1,0:T(8,128)(2,1)}, u32[]{:S(2)}) copy-start(bf16[256,1024]{1,0:T(8,128)(2,1)} %v_ref.1) | copy-start | bytes 1572868
  3.1 0.8 %copy-start.3 = (bf16[256,128]{1,0:T(8,128)(2,1)S(1)}, bf16[256,128]{1,0:T(8,128)(2,1)}, u32[]{:S(2)}) copy-start(bf16[256,128]{1,0:T(8,128)(2,1)} %qb_ref.1) | copy-start | bytes 196612
  4.0 0.8 %copy-start.4 = (bf16[256,128]{1,0:T(8,128)(2,1)S(1)}, bf16[256,128]{1,0:T(8,128)(2,1)}, u32[]{:S(2)}) copy-start(bf16[256,128]{1,0:T(8,128)(2,1)} %kb_ref.1) | copy-start | bytes 196612
  4.8 0.7 %copy-start.5 = (f32[1024]{0:T(1024)S(1)}, f32[1024]{0:T(1024)}, u32[]{:S(2)}) copy-start(f32[1024]{0:T(1024)} %param.11) | copy-start | bytes 12292

commit v2 on v1

--- a/solution.py
+++ b/solution.py
@@ -41,8 +41,8 @@
     return jnp.where(c >= LIN, 0.5, scale).astype(F32)
 
 
-def kernel(n, heads, q_ref, k_ref, v_ref, qb_ref, kb_ref, gain_ref, out_ref,
-           khalo, vhalo, prior, onward, state, qfeat, top, total, owin, lin,
+def kernel(n, heads, q_hbm, k_hbm, v_hbm, qb_hbm, kb_hbm, gain_hbm, out_ref,
+           q_ref, k_ref, v_ref, qb_ref, kb_ref, gain_ref, loads, khalo, vhalo, prior, onward, state, qfeat, top, total, owin, lin,
            ksend, vsend, psend, krecv, vrecv, precv):
     me = lax.axis_index("seq")
     tokens = q_ref.shape[0]
@@ -51,11 +51,17 @@
     nxt = {"seq": jnp.minimum(me + 1, n - 1)}
     prv = {"seq": jnp.maximum(me - 1, 0)}
 
+    pairs = ((kb_hbm, kb_ref), (v_hbm, v_ref), (k_hbm, k_ref), (qb_hbm, qb_ref), (q_hbm, q_ref),
+             (gain_hbm, gain_ref))
+    fetches = [pltpu.make_async_copy(a, b, loads.at[at]) for at, (a, b) in enumerate(pairs)]
     barrier = pltpu.get_barrier_semaphore()
 
     @pl.when(has_prev)
     def _():
         pl.semaphore_signal(barrier, inc=1, device_id=prv, device_id_type=pl.DeviceIdType.MESH)
+
+    for fetch in fetches:
+        fetch.start()
 
     @pl.when(me == 0)
     def _():
@@ -68,16 +74,16 @@
         pl.semaphore_wait(barrier, 1)
 
     def cols(h):
-        return pl.ds(pl.multiple_of(h * DH, DH), DH)
+        return pl.ds(h * DH, DH)
 
     def kcopy(h):
         return pltpu.make_async_remote_copy(
-            src_ref=k_ref.at[:, cols(h)], dst_ref=khalo.at[h], send_sem=ksend.at[h],
+            src_ref=k_hbm.at[:, cols(h)], dst_ref=khalo.at[h], send_sem=ksend.at[h],
             recv_sem=krecv.at[h], device_id=nxt, device_id_type=pl.DeviceIdType.MESH)
 
     def vcopy(h):
         return pltpu.make_async_remote_copy(
-            src_ref=v_ref.at[:, cols(h)], dst_ref=vhalo.at[h], send_sem=vsend.at[h],
+            src_ref=v_hbm.at[:, cols(h)], dst_ref=vhalo.at[h], send_sem=vsend.at[h],
             recv_sem=vrecv.at[h], device_id=nxt, device_id_type=pl.DeviceIdType.MESH)
 
     def pcopy(h):
@@ -86,10 +92,8 @@
             recv_sem=precv.at[h], device_id=nxt, device_id_type=pl.DeviceIdType.MESH)
 
     def each_head(body):
-        def step(h, carry):
+        for h in range(heads):
             body(h)
-            return carry
-        lax.fori_loop(0, heads, step, 0)
 
     crow = lax.broadcasted_iota(jnp.int32, (ROWS, heads * FD), 0)
     lane = lax.broadcasted_iota(jnp.int32, (ROWS, heads * FD), 1)
@@ -107,15 +111,18 @@
         a = dot_nt(pick_a, kb_ref[...]) + kone_a
         b = dot_nt(pick_b, kb_ref[...]) + kone_b
         feats = (a * b * kscale).astype(BF16)
-        got = dot_nn(feats, v_ref[:, cols(h)])
-        state[h] = got
-
-        @pl.when(me == 0)
-        def _():
-            onward[h] = got.astype(onward.dtype)
+        state[h] = dot_nn(feats, v_ref[:, cols(h)])
+
+    fetches[0].wait()
+    fetches[1].wait()
+    each_head(own_state)
+
+    @pl.when(me == 0)
+    def _():
+        def send(h):
+            onward[h] = state[h].astype(onward.dtype)
             pcopy(h).start()
-
-    each_head(own_state)
+        each_head(send)
 
     @pl.when(has_next)
     def _():
@@ -172,6 +179,8 @@
         b = dot_nn(qb, pick_b) + qone_b
         qfeat[h] = (a * b * qscale).astype(BF16)
 
+    for fetch in fetches[2:]:
+        fetch.wait()
     each_head(local)
 
     @pl.when(me > early)
@@ -181,11 +190,6 @@
     reach = jnp.where(has_prev, 0, tokens)
 
     def finish(h):
-        @pl.when(has_prev)
-        def _():
-            kcopy(h).wait_recv()
-            vcopy(h).wait_recv()
-
         scores = dot_nt(q_ref[:, cols(h)], khalo[h]) * root
         scores = jnp.where(col >= row + reach, scores, NEG)
         before = top[h]
@@ -198,7 +202,18 @@
         inv = lax.rsqrt(jnp.mean(raw * raw, axis=-1, keepdims=True) + 1e-05)
         out_ref[:, cols(h)] = (window + raw * inv * gain_ref[:, cols(h)]).astype(BF16)
 
-    each_head(finish)
+    group = 2
+    for begin in range(0, heads, group):
+        members = range(begin, min(begin + group, heads))
+
+        @pl.when(has_prev)
+        def _():
+            for h in members:
+                kcopy(h).wait_recv()
+                vcopy(h).wait_recv()
+
+        for h in members:
+            finish(h)
 
     @pl.when(has_next)
     def _():
@@ -222,9 +237,16 @@
         return pl.pallas_call(
             functools.partial(kernel, n, heads),
             out_shape=jax.ShapeDtypeStruct((tokens, width), BF16),
-            in_specs=[vmem] * 6,
+            in_specs=[pl.BlockSpec(memory_space=pltpu.HBM)] * 6,
             out_specs=vmem,
             scratch_shapes=[
+                pltpu.VMEM((tokens, width), BF16),
+                pltpu.VMEM((tokens, width), BF16),
+                pltpu.VMEM((tokens, width), BF16),
+                pltpu.VMEM(query_basis.shape, BF16),
+                pltpu.VMEM(key_basis.shape, BF16),
+                pltpu.VMEM((1, width), F32),
+                pltpu.SemaphoreType.DMA((6,)),
                 pltpu.VMEM((heads, tokens, DH), BF16),
                 pltpu.VMEM((heads, tokens, DH), BF16),
                 pltpu.VMEM((heads, ROWS, DH), carried),

time: 62.7 us -> 62 us (0.989)
    pallas_call x1, Pallas kernels: 56 us -> 55.4 us  [on_device(): pl.pallas_call(functools.partial(kernel, n, heads), out_shape=jax.ShapeDt...]
where the time goes in v2:
time: 62 us; the launch traced here: 61.7 us
  Pallas kernels  55.4 us (89%)
  local copies, waits for them, and re-layouts  6.28 us (10%)
    pallas_call x1, Pallas kernels, on_device(): pl.pallas_call(functools.partial(kernel, n, heads), out_shape=jax.ShapeDt...  55.4 us
    unnamed x13, local copies, waits for them, and re-layouts  6.28 us

profile of v2, /device:TPU:26, one launch (start us, length us, event | category | flops | bytes accessed | tf_op | source)
XLA Modules:
  0.0 61.7 jit_solution(3178521251805199084)
XLA Ops:
  0.0 0.0 copy-start
  0.0 1.0 %copy-done = bf16[256,1024]{1,0:T(8,128)(2,1)S(1)} copy-done((bf16[256,1024]{1,0:T(8,128)(2,1)S(1)}, bf16[256,1024]{1,0:T(8,128)(2,1)}, u32[]{:S(2)}) %copy-start) | copy-done | bytes 524312
  1.0 0.0 copy-start.1
  1.0 1.0 %copy-done.1 = bf16[256,1024]{1,0:T(8,128)(2,1)S(1)} copy-done((bf16[256,1024]{1,0:T(8,128)(2,1)S(1)}, bf16[256,1024]{1,0:T(8,128)(2,1)}, u32[]{:S(2)}) %copy-start.1) | copy-done | bytes 524312
  2.1 0.0 copy-start.2
  2.1 1.0 %copy-done.2 = bf16[256,1024]{1,0:T(8,128)(2,1)S(1)} copy-done((bf16[256,1024]{1,0:T(8,128)(2,1)S(1)}, bf16[256,1024]{1,0:T(8,128)(2,1)}, u32[]{:S(2)}) %copy-start.2) | copy-done | bytes 524312
  3.1 0.0 copy-start.3
  3.1 0.8 %copy-done.3 = bf16[256,128]{1,0:T(8,128)(2,1)S(1)} copy-done((bf16[256,128]{1,0:T(8,128)(2,1)S(1)}, bf16[256,128]{1,0:T(8,128)(2,1)}, u32[]{:S(2)}) %copy-start.3) | copy-done | bytes 65560
  4.0 0.0 copy-start.4
  4.0 0.8 %copy-done.4 = bf16[256,128]{1,0:T(8,128)(2,1)S(1)} copy-done((bf16[256,128]{1,0:T(8,128)(2,1)S(1)}, bf16[256,128]{1,0:T(8,128)(2,1)}, u32[]{:S(2)}) %copy-start.4) | copy-done | bytes 65560
  4.8 0.0 copy-start.5
  4.8 0.7 %copy-done.5 = f32[1024]{0:T(1024)S(1)} copy-done((f32[1024]{0:T(1024)S(1)}, f32[1024]{0:T(1024)}, u32[]{:S(2)}) %copy-start.5) | copy-done | bytes 4120
  5.5 55.4 %shard_map.64 = bf16[256,1024]{1,0:T(8,128)(2,1)S(1)} custom-call(bf16[256,1024]{1,0:T(8,128)(2,1)S(1)} %copy-done, bf16[256,1024]{1,0:T(8,128)(2,1)S(1)} %copy-done.1, bf16[256,1024]{1,0:T(8,128)(2,1)S(1)} %copy-done.2, bf16[256,128]{1,0:T(8,128)(2,1)S(1)} %copy-done.3, bf16[256,128]{1,0:T(8,128)(2,1)S(1)} %copy-done.4, f32[1,1024]{1,0:T(1,128)S(1)} %bitcast.1), custom_call_target="tpu_custom_call" | custom-call | flops 1174405120 | bytes 2097152 | tf_op jit(solution)/shard_map/pallas_call | solution.py:237
  60.9 0.8 %copy.8 = bf16[256,1024]{1,0:T(8,128)(2,1)} copy(bf16[256,1024]{1,0:T(8,128)(2,1)S(1)} %shard_map.64) | data formatting | bytes 1048576
Async XLA Ops:
  0.0 1.0 %copy-start = (bf16[256,1024]{1,0:T(8,128)(2,1)S(1)}, bf16[256,1024]{1,0:T(8,128)(2,1)}, u32[]{:S(2)}) copy-start(bf16[256,1024]{1,0:T(8,128)(2,1)} %q_hbm.1) | copy-start | bytes 1572868
  1.0 1.0 %copy-start.1 = (bf16[256,1024]{1,0:T(8,128)(2,1)S(1)}, bf16[256,1024]{1,0:T(8,128)(2,1)}, u32[]{:S(2)}) copy-start(bf16[256,1024]{1,0:T(8,128)(2,1)} %k_hbm.1) | copy-start | bytes 1572868
  2.1 1.0 %copy-start.2 = (bf16[256,1024]{1,0:T(8,128)(2,1)S(1)}, bf16[256,1024]{1,0:T(8,128)(2,1)}, u32[]{:S(2)}) copy-start(bf16[256,1024]{1,0:T(8,128)(2,1)} %v_hbm.1) | copy-start | bytes 1572868
  3.1 0.8 %copy-start.3 = (bf16[256,128]{1,0:T(8,128)(2,1)S(1)}, bf16[256,128]{1,0:T(8,128)(2,1)}, u32[]{:S(2)}) copy-start(bf16[256,128]{1,0:T(8,128)(2,1)} %qb_hbm.1) | copy-start | bytes 196612
  4.0 0.8 %copy-start.4 = (bf16[256,128]{1,0:T(8,128)(2,1)S(1)}, bf16[256,128]{1,0:T(8,128)(2,1)}, u32[]{:S(2)}) copy-start(bf16[256,128]{1,0:T(8,128)(2,1)} %kb_hbm.1) | copy-start | bytes 196612
  4.8 0.7 %copy-start.5 = (f32[1024]{0:T(1024)S(1)}, f32[1024]{0:T(1024)}, u32[]{:S(2)}) copy-start(f32[1024]{0:T(1024)} %param.11) | copy-start | bytes 12292

commit v3 on v2

--- a/solution.py
+++ b/solution.py
@@ -113,23 +113,34 @@
         feats = (a * b * kscale).astype(BF16)
         state[h] = dot_nn(feats, v_ref[:, cols(h)])
 
+    ahead = me - 1
+
+    def send_halo(h, now):
+        @pl.when(has_next & now)
+        def _():
+            kcopy(h).start()
+            vcopy(h).start()
+
+    for h in range(heads):
+        send_halo(h, h < ahead)
+
     fetches[0].wait()
     fetches[1].wait()
-    each_head(own_state)
+    for begin in range(0, heads, 4):
+        members = range(begin, min(begin + 4, heads))
+        for h in members:
+            own_state(h)
+
+        @pl.when((me == 0) & has_next)
+        def _():
+            for h in members:
+                onward[h] = state[h].astype(onward.dtype)
+                pcopy(h).start()
 
     @pl.when(me == 0)
     def _():
-        def send(h):
-            onward[h] = state[h].astype(onward.dtype)
-            pcopy(h).start()
-        each_head(send)
-
-    @pl.when(has_next)
-    def _():
-        def send(h):
-            kcopy(h).start()
-            vcopy(h).start()
-        each_head(send)
+        for h in range(heads):
+            send_halo(h, True)
 
     def chain(h):
         pcopy(h).wait_recv()
@@ -144,6 +155,8 @@
     @pl.when(has_prev & (me <= early))
     def _():
         each_head(chain)
+        for h in range(heads):
+            send_halo(h, h >= ahead)
 
     row = lax.broadcasted_iota(jnp.int32, (tokens, tokens), 0)
     col = lax.broadcasted_iota(jnp.int32, (tokens, tokens), 1)
@@ -186,6 +199,8 @@
     @pl.when(me > early)
     def _():
         each_head(chain)
+        for h in range(heads):
+            send_halo(h, h >= ahead)
 
     reach = jnp.where(has_prev, 0, tokens)
 
@@ -260,7 +275,7 @@
                 dma, dma, dma, dma, dma, dma,
             ],
             compiler_params=pltpu.CompilerParams(
-                collective_id=0, has_side_effects=True, vmem_limit_bytes=40 * 2**20),
+                collective_id=0, has_side_effects=True, vmem_limit_bytes=63 * 2**20),
             cost_estimate=pl.CostEstimate(
                 flops=flops, bytes_accessed=8 * tokens * width, transcendentals=2 * tokens * tokens * heads),
         )(queries, key_rows, value_rows, query_basis, key_basis, linear_gain.reshape(1, width))

time: 62 us -> 41.4 us (0.67)
  Pallas kernels: 55.4 us -> 39.2 us
  local copies, waits for them, and re-layouts: 6.28 us -> 1.87 us
    pallas_call x1, Pallas kernels: 55.4 us -> 39.2 us  [on_device(): pl.pallas_call(functools.partial(kernel, n, heads), out_shape=jax.ShapeDt...]
    unnamed x13 -> x1, local copies, waits for them, and re-layouts: 6.28 us -> 1.87 us
where the time goes in v3:
time: 41.4 us; the launch traced here: 41.1 us
  Pallas kernels  39.2 us (95%)
  local copies, waits for them, and re-layouts  1.87 us (5%)
    pallas_call x1, Pallas kernels, on_device(): pl.pallas_call(functools.partial(kernel, n, heads), out_shape=jax.ShapeDt...  39.2 us
    unnamed x1, local copies, waits for them, and re-layouts  1.87 us

profile of v3, /device:TPU:26, one launch (start us, length us, event | category | flops | bytes accessed | tf_op | source)
XLA Modules:
  0.0 41.1 jit_solution(13832085330943201265)
XLA Ops:
  0.0 39.2 %shard_map.64 = bf16[256,1024]{1,0:T(8,128)(2,1)} custom-call(bf16[256,1024]{1,0:T(8,128)(2,1)} %q_hbm.1, bf16[256,1024]{1,0:T(8,128)(2,1)} %k_hbm.1, bf16[256,1024]{1,0:T(8,128)(2,1)} %v_hbm.1, bf16[256,128]{1,0:T(8,128)(2,1)} %qb_hbm.1, bf16[256,128]{1,0:T(8,128)(2,1)} %kb_hbm.1, f32[1,1024]{1,0:T(1,128)} %bitcast.1), custom_call_target="tpu_custom_call" | custom-call | flops 1174405120 | bytes 2097152 | tf_op jit(solution)/shard_map/pallas_call | solution.py:252
  39.2 1.9 %copy.8 = bf16[256,1024]{1,0:T(8,128)(2,1)} copy(bf16[256,1024]{1,0:T(8,128)(2,1)} %shard_map.64) | data formatting | bytes 1048576

commit v4 on v2

--- a/solution.py
+++ b/solution.py
@@ -42,23 +42,32 @@
 
 
 def kernel(n, heads, q_hbm, k_hbm, v_hbm, qb_hbm, kb_hbm, gain_hbm, out_ref,
-           q_ref, k_ref, v_ref, qb_ref, kb_ref, gain_ref, loads, khalo, vhalo, prior, onward, state, qfeat, top, total, owin, lin,
-           ksend, vsend, psend, krecv, vrecv, precv):
+           q_ref, k_ref, v_ref, qb_ref, kb_ref, gain_ref, loads, khalo, vhalo, bhalo, relay,
+           carry, onward, prior, state, qfeat, top, total, owin, lin, bsend, brecv,
+           ksend, vsend, psend, krecv, vrecv, precv, rsend, rrecv, fsend):
     me = lax.axis_index("seq")
     tokens = q_ref.shape[0]
     has_next = me < n - 1
     has_prev = me > 0
-    nxt = {"seq": jnp.minimum(me + 1, n - 1)}
-    prv = {"seq": jnp.maximum(me - 1, 0)}
+    even = lax.rem(me, 2) == 0
+    has_after = me + 2 < n
+    relays = even & has_after
+    relayed_out = (~even) & has_next
+    relayed = relay.shape[0]
+    mesh_ids = pl.DeviceIdType.MESH
+
+    def at(distance):
+        return {"seq": jnp.clip(me + distance, 0, n - 1)}
 
     pairs = ((kb_hbm, kb_ref), (v_hbm, v_ref), (k_hbm, k_ref), (qb_hbm, qb_ref), (q_hbm, q_ref),
              (gain_hbm, gain_ref))
-    fetches = [pltpu.make_async_copy(a, b, loads.at[at]) for at, (a, b) in enumerate(pairs)]
+    fetches = [pltpu.make_async_copy(a, b, loads.at[slot]) for slot, (a, b) in enumerate(pairs)]
     barrier = pltpu.get_barrier_semaphore()
 
-    @pl.when(has_prev)
-    def _():
-        pl.semaphore_signal(barrier, inc=1, device_id=prv, device_id_type=pl.DeviceIdType.MESH)
+    for distance, sends in ((-1, has_prev), (-2, me >= 2), (1, relays)):
+        @pl.when(sends)
+        def _():
+            pl.semaphore_signal(barrier, inc=1, device_id=at(distance), device_id_type=mesh_ids)
 
     for fetch in fetches:
         fetch.start()
@@ -67,33 +76,55 @@
     def _():
         khalo[...] = jnp.zeros_like(khalo)
         vhalo[...] = jnp.zeros_like(vhalo)
-        prior[...] = jnp.zeros_like(prior)
+        bhalo[...] = jnp.zeros_like(bhalo)
+
+    @pl.when(me < 2)
+    def _():
+        carry[...] = jnp.zeros_like(carry)
 
     @pl.when(has_next)
     def _():
-        pl.semaphore_wait(barrier, 1)
+        reached = 1 + has_after.astype(jnp.int32) + relayed_out.astype(jnp.int32)
+        pl.semaphore_wait(barrier, reached)
 
     def cols(h):
         return pl.ds(h * DH, DH)
 
+    def remote(src, dst, send, recv, distance):
+        return pltpu.make_async_remote_copy(
+            src_ref=src, dst_ref=dst, send_sem=send, recv_sem=recv, device_id=at(distance),
+            device_id_type=mesh_ids)
+
+    def bcopy():
+        return remote(kb_hbm, bhalo, bsend.at[0], brecv.at[0], 1)
+
     def kcopy(h):
-        return pltpu.make_async_remote_copy(
-            src_ref=k_hbm.at[:, cols(h)], dst_ref=khalo.at[h], send_sem=ksend.at[h],
-            recv_sem=krecv.at[h], device_id=nxt, device_id_type=pl.DeviceIdType.MESH)
+        return remote(k_hbm.at[:, cols(h)], khalo.at[h], ksend.at[h], krecv.at[h], 1)
 
     def vcopy(h):
-        return pltpu.make_async_remote_copy(
-            src_ref=v_hbm.at[:, cols(h)], dst_ref=vhalo.at[h], send_sem=vsend.at[h],
-            recv_sem=vrecv.at[h], device_id=nxt, device_id_type=pl.DeviceIdType.MESH)
+        return remote(v_hbm.at[:, cols(h)], vhalo.at[h], vsend.at[h], vrecv.at[h], 1)
 
     def pcopy(h):
-        return pltpu.make_async_remote_copy(
-            src_ref=onward.at[h], dst_ref=prior.at[h], send_sem=psend.at[h],
-            recv_sem=precv.at[h], device_id=nxt, device_id_type=pl.DeviceIdType.MESH)
+        return remote(onward.at[h], carry.at[h], psend.at[h], precv.at[h], 2)
+
+    def rcopy(h):
+        return remote(k_hbm.at[:, cols(h)], relay.at[h], rsend.at[h], rrecv.at[h], -1)
+
+    def fcopy(h):
+        return remote(relay.at[h], khalo.at[h], fsend.at[h], krecv.at[h], 2)
 
     def each_head(body):
         for h in range(heads):
             body(h)
+
+    @pl.when(has_next)
+    def _():
+        bcopy().start()
+
+    @pl.when(has_next)
+    def _():
+        for h in range(heads):
+            vcopy(h).start()
 
     crow = lax.broadcasted_iota(jnp.int32, (ROWS, heads * FD), 0)
     lane = lax.broadcasted_iota(jnp.int32, (ROWS, heads * FD), 1)
@@ -105,45 +136,28 @@
     kone_a = jnp.where(ccol == ONE, 1.0, 0.0).astype(F32)
     kone_b = jnp.where(ccol >= ONE, 1.0, 0.0).astype(F32)
 
-    def own_state(h):
+    def state_of(h, basis, values):
         pick_a = jnp.where(first == h * FD, 1.0, 0.0).astype(BF16)
         pick_b = jnp.where(second == h * FD, 1.0, 0.0).astype(BF16)
-        a = dot_nt(pick_a, kb_ref[...]) + kone_a
-        b = dot_nt(pick_b, kb_ref[...]) + kone_b
+        a = dot_nt(pick_a, basis) + kone_a
+        b = dot_nt(pick_b, basis) + kone_b
         feats = (a * b * kscale).astype(BF16)
-        state[h] = dot_nn(feats, v_ref[:, cols(h)])
+        return dot_nn(feats, values)
+
+    @pl.when(even & has_next)
+    def _():
+        for h in range(heads):
+            kcopy(h).start()
+
+    @pl.when(relayed_out)
+    def _():
+        for h in range(relayed):
+            rcopy(h).start()
 
     fetches[0].wait()
     fetches[1].wait()
-    each_head(own_state)
-
-    @pl.when(me == 0)
-    def _():
-        def send(h):
-            onward[h] = state[h].astype(onward.dtype)
-            pcopy(h).start()
-        each_head(send)
-
-    @pl.when(has_next)
-    def _():
-        def send(h):
-            kcopy(h).start()
-            vcopy(h).start()
-        each_head(send)
-
-    def chain(h):
-        pcopy(h).wait_recv()
-
-        @pl.when(has_next)
-        def _():
-            onward[h] = (prior[h].astype(F32) + state[h]).astype(onward.dtype)
-            pcopy(h).start()
-
-    early = n // 2 - 1
-
-    @pl.when(has_prev & (me <= early))
-    def _():
-        each_head(chain)
+    for h in range(heads):
+        state[h] = state_of(h, kb_ref[...], v_ref[:, cols(h)])
 
     row = lax.broadcasted_iota(jnp.int32, (tokens, tokens), 0)
     col = lax.broadcasted_iota(jnp.int32, (tokens, tokens), 1)
@@ -183,9 +197,39 @@
         fetch.wait()
     each_head(local)
 
-    @pl.when(me > early)
-    def _():
-        each_head(chain)
+    @pl.when(has_prev)
+    def _():
+        bcopy().wait_recv()
+
+    for h in range(heads):
+        @pl.when(has_prev)
+        def _():
+            vcopy(h).wait_recv()
+
+        between = state_of(h, bhalo[...], vhalo[h])
+
+        @pl.when(me >= 2)
+        def _():
+            pcopy(h).wait_recv()
+
+        before = carry[h].astype(F32) + between
+        prior[h] = before.astype(BF16)
+
+        @pl.when(has_after)
+        def _():
+            onward[h] = (before + state[h]).astype(onward.dtype)
+            pcopy(h).start()
+
+    @pl.when(relays)
+    def _():
+        for h in range(relayed):
+            rcopy(h).wait_recv()
+            fcopy(h).start()
+
+    @pl.when(relayed_out)
+    def _():
+        for h in range(relayed, heads):
+            kcopy(h).start()
 
     reach = jnp.where(has_prev, 0, tokens)
 
@@ -198,7 +242,7 @@
         shrink = jnp.exp(before - peak)
         full = total[h] * shrink + jnp.sum(expo, axis=-1, keepdims=True)
         window = (owin[h] * shrink + dot_nn(expo.astype(BF16), vhalo[h])) / full
-        raw = lin[h] + dot_nn(qfeat[h], prior[h].astype(BF16))
+        raw = lin[h] + dot_nn(qfeat[h], prior[h])
         inv = lax.rsqrt(jnp.mean(raw * raw, axis=-1, keepdims=True) + 1e-05)
         out_ref[:, cols(h)] = (window + raw * inv * gain_ref[:, cols(h)]).astype(BF16)
 
@@ -210,18 +254,37 @@
         def _():
             for h in members:
                 kcopy(h).wait_recv()
-                vcopy(h).wait_recv()
 
         for h in members:
             finish(h)
 
     @pl.when(has_next)
     def _():
-        def sent(h):
+        bcopy().wait_send()
+        for h in range(heads):
+            vcopy(h).wait_send()
+        for h in range(relayed, heads):
             kcopy(h).wait_send()
-            vcopy(h).wait_send()
+
+    @pl.when(even & has_next)
+    def _():
+        for h in range(relayed):
+            kcopy(h).wait_send()
+
+    @pl.when(relayed_out)
+    def _():
+        for h in range(relayed):
+            rcopy(h).wait_send()
+
+    @pl.when(relays)
+    def _():
+        for h in range(relayed):
+            fcopy(h).wait_send()
+
+    @pl.when(has_after)
+    def _():
+        for h in range(heads):
             pcopy(h).wait_send()
-        each_head(sent)
 
 
 def solution(mesh):
@@ -249,18 +312,23 @@
                 pltpu.SemaphoreType.DMA((6,)),
                 pltpu.VMEM((heads, tokens, DH), BF16),
                 pltpu.VMEM((heads, tokens, DH), BF16),
+                pltpu.VMEM(key_basis.shape, BF16),
+                pltpu.VMEM((max(heads * 3 // 8, 1), tokens, DH), BF16),
                 pltpu.VMEM((heads, ROWS, DH), carried),
                 pltpu.VMEM((heads, ROWS, DH), carried),
+                pltpu.VMEM((heads, ROWS, DH), BF16),
                 pltpu.VMEM((heads, ROWS, DH), F32),
                 pltpu.VMEM((heads, tokens, ROWS), BF16),
                 pltpu.VMEM((heads, tokens, 1), F32),
                 pltpu.VMEM((heads, tokens, 1), F32),
                 pltpu.VMEM((heads, tokens, DH), F32),
                 pltpu.VMEM((heads, tokens, DH), F32),
-                dma, dma, dma, dma, dma, dma,
+                pltpu.SemaphoreType.DMA((1,)),
+                pltpu.SemaphoreType.DMA((1,)),
+                dma, dma, dma, dma, dma, dma, dma, dma, dma,
             ],
             compiler_params=pltpu.CompilerParams(
-                collective_id=0, has_side_effects=True, vmem_limit_bytes=40 * 2**20),
+                collective_id=0, has_side_effects=True, vmem_limit_bytes=63 * 2**20),
             cost_estimate=pl.CostEstimate(
                 flops=flops, bytes_accessed=8 * tokens * width, transcendentals=2 * tokens * tokens * heads),
         )(queries, key_rows, value_rows, query_basis, key_basis, linear_gain.reshape(1, width))

time: 62 us -> 40.5 us (0.65)
  the two profiles are of different devices: /device:TPU:26 before, /device:TPU:24 now
where the time goes in v4:
time: 40.5 us; the launch traced here: 40.3 us
  Pallas kernels  38.4 us (95%)
  local copies, waits for them, and re-layouts  1.87 us (5%)
    pallas_call x1, Pallas kernels, on_device(): pl.pallas_call(functools.partial(kernel, n, heads), out_shape=jax.ShapeDt...  38.4 us
    unnamed x1, local copies, waits for them, and re-layouts  1.87 us

profile of v4, /device:TPU:24, one launch (start us, length us, event | category | flops | bytes accessed | tf_op | source)
XLA Modules:
  0.0 40.3 jit_solution(782551709093833125)
XLA Ops:
  0.0 38.4 %shard_map.64 = bf16[256,1024]{1,0:T(8,128)(2,1)} custom-call(bf16[256,1024]{1,0:T(8,128)(2,1)} %q_hbm.1, bf16[256,1024]{1,0:T(8,128)(2,1)} %k_hbm.1, bf16[256,1024]{1,0:T(8,128)(2,1)} %v_hbm.1, bf16[256,128]{1,0:T(8,128)(2,1)} %qb_hbm.1, bf16[256,128]{1,0:T(8,128)(2,1)} %kb_hbm.1, f32[1,1024]{1,0:T(1,128)} %bitcast.1), custom_call_target="tpu_custom_call" | custom-call | flops 1174405120 | bytes 2097152 | tf_op jit(solution)/shard_map/pallas_call | solution.py:300
  38.4 1.9 %copy.8 = bf16[256,1024]{1,0:T(8,128)(2,1)} copy(bf16[256,1024]{1,0:T(8,128)(2,1)} %shard_map.64) | data formatting | bytes 1048576
